TPU v7x, 256 devices: a whole 4x4x8 slice. The times are simulated.
256 devices in a mesh: col: 32 (over x, z), row: 8 (over y, core).
Axes of the slice: x: 4, y: 4, z: 8, core: 2. Of those that a mesh axis runs over, the one named last changes fastest.
Arguments:
- matrix: float32 [8192, 8192], P('row', 'col'), as said below
- flips: int32 [4, 32], P(None, 'col'), may hold values 0 or 1
Outputs:
- rotated: float32 [8192, 8192], P('row', 'col')
Inputs may be any that keep to these rules, and one draw needn't show every extreme that they name: `matrix`: dense real-valued activations.
All inputs are finite; a program needn't handle non-finite values. No bound on the sum of `flips` on one device may be relied on, other than what follows from the above.
Results may differ from a plain program's by a relative error of at most 0.0003.
Values sent between devices are 32-bit elements; how exact they have to be, the bound alone decides.
A program may use at most 64 MiB of HBM per device.

v0:
```python
import jax
import jax.numpy as jnp
from jax import lax
from jax.sharding import PartitionSpec as P

ROUNDS = 4
STEPS = 8


HIGH = lax.Precision.HIGHEST


def passed_along(array, axis, by):
    count = lax.axis_size(axis)
    pairs = [(i, i + by) for i in range(count) if 0 <= i + by < count]
    return lax.ppermute(array, axis, pairs)


def matmul(leading, trailing):
    return jnp.dot(leading, trailing, precision=HIGH, preferred_element_type=jnp.float32)


def inner_rows(leading, trailing):
    return lax.dot_general(
        leading,
        trailing,
        (((0,), (0,)), ((), ())),
        precision=HIGH,
        preferred_element_type=jnp.float32,
    )


def reorder_columns(values, width):
    return jnp.concatenate(
        [
            values[:, 0:1],
            values[:, width : width + 1],
            values[:, 1 : width - 1],
            values[:, width + 1 :],
            values[:, width - 1 : width],
        ],
        axis=1,
    )


def reorder_rows(values, width):
    return jnp.concatenate(
        [
            values[0:1],
            values[width : width + 1],
            values[1 : width - 1],
            values[width + 1 :],
            values[width - 1 : width],
        ],
        axis=0,
    )


def turn_pair(gram, basis):
    width = gram.shape[0] // 2
    diagonal_now = jnp.diagonal(gram)
    first = diagonal_now[:width]
    second = diagonal_now[width:]
    cross = jnp.diagonal(gram[:width, width:])
    differ = second - first
    sign_part = jnp.where(differ >= 0, 1.0, -1.0)
    tangent = (
        2.0
        * cross
        * sign_part
        / (
            jnp.abs(differ)
            + jnp.sqrt(differ * differ + 4.0 * cross * cross)
            + 1e-06 * (first + second)
        )
    )
    cosine = 1.0 / jnp.sqrt(1.0 + tangent * tangent)
    sine_term = cosine * tangent

    def columns(values):
        leading = values[:, :width]
        trailing = values[:, width:]
        return jnp.concatenate(
            [leading * cosine - trailing * sine_term, leading * sine_term + trailing * cosine],
            axis=1,
        )

    gram = columns(gram)
    leading = gram[:width]
    trailing = gram[width:]
    gram = jnp.concatenate(
        [
            leading * cosine[:, None] - trailing * sine_term[:, None],
            leading * sine_term[:, None] + trailing * cosine[:, None],
        ],
        axis=0,
    )
    basis = columns(basis)
    gram = reorder_rows(reorder_columns(gram, width), width)
    basis = reorder_columns(basis, width)
    return (gram, basis)


def diagonalize(gram):
    basis = jnp.eye(gram.shape[0], dtype=jnp.float32)
    for inner in range(STEPS):
        gram, basis = turn_pair(gram, basis)
    return (basis, gram)


def full_gram(paired):
    return lax.psum(inner_rows(paired, paired), "row")


def move_plain(top_swapped, bottom_swapped, position, last):
    sending = jnp.where(position == 0, bottom_swapped, top_swapped)
    arrived = passed_along(sending, "col", 1)
    coming = passed_along(bottom_swapped, "col", -1)
    next_top = jnp.where(position == 0, top_swapped, arrived)
    next_bottom = jnp.where(position == last, top_swapped, coming)
    return (next_top, next_bottom)


def body(matrix, flips):
    width = matrix.shape[1] // 2
    position = lax.axis_index("col")
    last = lax.axis_size("col") - 1
    upper = matrix[:, :width]
    lower_half = matrix[:, width:]
    for round_index in range(ROUNDS):
        paired = jnp.concatenate([upper, lower_half], axis=1)
        gram = full_gram(paired)
        basis, settled = diagonalize(gram)
        paired = matmul(paired, basis)
        flipped = flips[round_index, 0] == 1
        top_swapped = jnp.where(flipped, paired[:, width:], paired[:, :width])
        bottom_swapped = jnp.where(flipped, paired[:, :width], paired[:, width:])
        upper, lower_half = move_plain(top_swapped, bottom_swapped, position, last)
    return jnp.concatenate([upper, lower_half], axis=1)


def solution(mesh):
    placed = (P("row", "col"), P(None, "col"))
    return jax.shard_map(
        body, mesh=mesh, in_specs=placed, out_specs=P("row", "col"), check_vma=False
    )
```

profile of v0, /device:TPU:120, one launch (start us, length us, event | category | flops | bytes accessed | tf_op | source)
XLA Modules:
  0.0 544.2 jit_solution(843958226854005357)
XLA Ops:
  7.8 2.5 fusion.374
  12.4 62.5 %all-reduce.5.cloned.1.call-done = f32[256,256]{1,0:T(8,128)} async-done(((f32[256,256]{1,0:T(8,128)}), f32[256,256]{1,0:T(8,128)}) %all-reduce.5.cloned.1.call-update) | async-done | bytes 262160 | tf_op jit(solution)/shard_map/psum | solution.py:112
  76.9 2.3 gather_fusion.1
  80.4 1.2 gather_fusion.2
  81.9 2.3 gather_fusion.3
  85.5 1.2 gather_fusion.4
  87.0 2.3 gather_fusion.5
  90.6 1.2 gather_fusion.6
  92.1 2.3 gather_fusion.7
  95.7 1.2 gather_fusion.8
  97.2 2.3 gather_fusion.9
  100.8 1.2 gather_fusion.10
  102.3 2.3 gather_fusion.11
  105.9 1.2 gather_fusion.12
  107.4 2.3 gather_fusion.13
  112.5 2.6 gather_fusion.15
  115.8 1.9 convolution_bitcast_fusion
  117.9 4.7 collective-permute-start
  122.5 1.9 collective-permute-start.1
  124.5 10.1 %collective-permute-done = f32[1024,128]{0,1:T(8,128)S(1)} collective-permute-done((f32[1024,128]{0,1:T(8,128)S(1)}, f32[1024,128]{0,1:T(8,128)S(1)}, u32[]{:S(2)}, u32[]{:S(2)}) %collective-permute-start) | collective-permute-done | bytes 524320 | tf_op jit(solution)/shard_map/ppermute | solution.py:16
  134.6 5.3 collective-permute-done.1
  141.9 1.7 fusion.5
  144.3 61.0 %all-reduce.7.cloned.1.call-done = f32[256,256]{1,0:T(8,128)} async-done(((f32[256,256]{1,0:T(8,128)}), f32[256,256]{1,0:T(8,128)}) %all-reduce.7.cloned.1.call-update) | async-done | bytes 262160 | tf_op jit(solution)/shard_map/psum | solution.py:112
  207.4 2.3 gather_fusion.17
  212.4 2.3 gather_fusion.19
  217.5 2.3 gather_fusion.21
  222.6 2.3 gather_fusion.23
  227.7 2.3 gather_fusion.25
  232.8 2.3 gather_fusion.27
  237.8 2.3 gather_fusion.29
  242.9 13.1 %gather_fusion.31 = f32[256]{0:T(256)S(1)} fusion(f32[256,256]{1,0:T(8,128)S(1)} %concatenate.811, s32[256]{0:T(256)S(1)} %bitcast.63), kind=kCustom, calls=%fused_computation.31 | custom fusion | bytes 4096 | tf_op jit(solution)/shard_map/jit(diagonal)/cond/branch_0_fun/gather | solution.py:61
  258.0 4.7 collective-permute-start.2
  262.7 1.9 collective-permute-start.3
  264.6 10.1 %collective-permute-done.2 = f32[1024,128]{0,1:T(8,128)S(1)} collective-permute-done((f32[1024,128]{0,1:T(8,128)S(1)}, f32[1024,128]{0,1:T(8,128)S(1)}, u32[]{:S(2)}, u32[]{:S(2)}) %collective-permute-start.2) | collective-permute-done | bytes 524320 | tf_op jit(solution)/shard_map/ppermute | solution.py:16
  274.8 5.3 collective-permute-done.3
  280.2 1.7 fusion.3
  282.7 60.9 %all-reduce.9.cloned.1.call-done = f32[256,256]{1,0:T(8,128)} async-done(((f32[256,256]{1,0:T(8,128)}), f32[256,256]{1,0:T(8,128)}) %all-reduce.9.cloned.1.call-update) | async-done | bytes 262160 | tf_op jit(solution)/shard_map/psum | solution.py:112
  345.7 2.3 gather_fusion.33
  350.7 2.3 gather_fusion.35
  355.8 2.3 gather_fusion.37
  360.9 2.3 gather_fusion.39
  366.0 2.3 gather_fusion.41
  371.1 2.3 gather_fusion.43
  376.1 2.3 gather_fusion.45
  381.2 2.6 gather_fusion.47
  385.8 4.7 collective-permute-start.4
  390.5 1.9 collective-permute-start.5
  392.4 10.1 %collective-permute-done.4 = f32[1024,128]{0,1:T(8,128)S(1)} collective-permute-done((f32[1024,128]{0,1:T(8,128)S(1)}, f32[1024,128]{0,1:T(8,128)S(1)}, u32[]{:S(2)}, u32[]{:S(2)}) %collective-permute-start.4) | collective-permute-done | bytes 524320 | tf_op jit(solution)/shard_map/ppermute | solution.py:16
  402.5 5.3 collective-permute-done.5
  408.0 1.7 fusion.1
  410.3 61.1 %all-reduce.11.cloned.1.call-done = f32[256,256]{1,0:T(8,128)} async-done(((f32[256,256]{1,0:T(8,128)}), f32[256,256]{1,0:T(8,128)}) %all-reduce.11.cloned.1.call-update) | async-done | bytes 262160 | tf_op jit(solution)/shard_map/psum | solution.py:112
  473.5 2.3 gather_fusion.49
  478.5 2.3 gather_fusion.51
  483.6 2.3 gather_fusion.53
  488.7 2.3 gather_fusion.55
  493.7 2.3 gather_fusion.57
  498.8 2.3 gather_fusion.59
  503.9 2.3 gather_fusion.61
  509.0 2.6 gather_fusion.63
  513.6 4.7 collective-permute-start.6
  518.3 1.9 collective-permute-start.7
  520.2 10.1 %collective-permute-done.6 = f32[1024,128]{0,1:T(8,128)S(1)} collective-permute-done((f32[1024,128]{0,1:T(8,128)S(1)}, f32[1024,128]{0,1:T(8,128)S(1)}, u32[]{:S(2)}, u32[]{:S(2)}) %collective-permute-start.6) | collective-permute-done | bytes 524320 | tf_op jit(solution)/shard_map/ppermute | solution.py:16
  530.4 5.3 collective-permute-done.7
  535.9 1.3 copy.4
  (546 shorter events, 85.7 us)
Async XLA Ops:
  6.5 1.2 copy-start
  6.5 68.3 %all-reduce.5.cloned.1.call-start = ((), (), s32[]{:S(2)}) async-start(), calls=%async_computation | async-start | bytes 524288 | tf_op jit(solution)/shard_map/psum | solution.py:112
  10.3 0.7 copy-start.7
  10.3 195.0 %all-reduce.7.cloned.1.call-start = ((), (), s32[]{:S(2)}) async-start(), calls=%async_computation.1 | async-start | bytes 524288 | tf_op jit(solution)/shard_map/psum | solution.py:112
  75.7 1.3 copy-start.2
  117.9 16.7 %collective-permute-start = (f32[1024,128]{0,1:T(8,128)S(1)}, f32[1024,128]{0,1:T(8,128)S(1)}, u32[]{:S(2)}, u32[]{:S(2)}) collective-permute-start(f32[1024,128]{0,1:T(8,128)S(1)} %get-tuple-element.62), channel_id=1, source_target_pairs={{0,8},{8,16},{16,24},{24,32},{32,40},{40,48},{48,56},{56,64},{64,7... | collective-permute-start | bytes 1572872 | tf_op jit(solution)/shard_map/ppermute | solution.py:16
  122.5 17.4 %collective-permute-start.1 = (f32[1024,128]{0,1:T(8,128)S(1)}, f32[1024,128]{0,1:T(8,128)S(1)}, u32[]{:S(2)}, u32[]{:S(2)}) collective-permute-start(f32[1024,128]{0,1:T(8,128)S(1)} %get-tuple-element.63), channel_id=1, source_target_pairs={{8,0},{16,8},{24,16},{32,24},{40,32},{48,40},{56,48},{64,56},{72,6... | collective-permute-start | bytes 1572872 | tf_op jit(solution)/shard_map/ppermute | solution.py:16
  139.9 0.8 copy-start.6
  143.7 199.9 %all-reduce.9.cloned.1.call-start = ((), (), s32[]{:S(2)}) async-start(), calls=%async_computation.2 | async-start | bytes 524288 | tf_op jit(solution)/shard_map/psum | solution.py:112
  206.2 1.3 copy-start.4
  258.0 16.7 %collective-permute-start.2 = (f32[1024,128]{0,1:T(8,128)S(1)}, f32[1024,128]{0,1:T(8,128)S(1)}, u32[]{:S(2)}, u32[]{:S(2)}) collective-permute-start(f32[1024,128]{0,1:T(8,128)S(1)} %get-tuple-element.43), channel_id=1, source_target_pairs={{0,8},{8,16},{16,24},{24,32},{32,40},{40,48},{48,56},{56,64},{64,7... | collective-permute-start | bytes 1572872 | tf_op jit(solution)/shard_map/ppermute | solution.py:16
  262.7 17.4 %collective-permute-start.3 = (f32[1024,128]{0,1:T(8,128)S(1)}, f32[1024,128]{0,1:T(8,128)S(1)}, u32[]{:S(2)}, u32[]{:S(2)}) collective-permute-start(f32[1024,128]{0,1:T(8,128)S(1)} %get-tuple-element.44), channel_id=1, source_target_pairs={{8,0},{16,8},{24,16},{32,24},{40,32},{48,40},{56,48},{64,56},{72,6... | collective-permute-start | bytes 1572872 | tf_op jit(solution)/shard_map/ppermute | solution.py:16
  282.0 189.4 %all-reduce.11.cloned.1.call-start = ((), (), s32[]{:S(2)}) async-start(), calls=%async_computation.3 | async-start | bytes 524288 | tf_op jit(solution)/shard_map/psum | solution.py:112
  344.5 1.3 copy-start.5
  385.8 16.7 %collective-permute-start.4 = (f32[1024,128]{0,1:T(8,128)S(1)}, f32[1024,128]{0,1:T(8,128)S(1)}, u32[]{:S(2)}, u32[]{:S(2)}) collective-permute-start(f32[1024,128]{0,1:T(8,128)S(1)} %get-tuple-element.24), channel_id=1, source_target_pairs={{0,8},{8,16},{16,24},{24,32},{32,40},{40,48},{48,56},{56,64},{64,7... | collective-permute-start | bytes 1572872 | tf_op jit(solution)/shard_map/ppermute | solution.py:16
  390.5 17.4 %collective-permute-start.5 = (f32[1024,128]{0,1:T(8,128)S(1)}, f32[1024,128]{0,1:T(8,128)S(1)}, u32[]{:S(2)}, u32[]{:S(2)}) collective-permute-start(f32[1024,128]{0,1:T(8,128)S(1)} %get-tuple-element.25), channel_id=1, source_target_pairs={{8,0},{16,8},{24,16},{32,24},{40,32},{48,40},{56,48},{64,56},{72,6... | collective-permute-start | bytes 1572872 | tf_op jit(solution)/shard_map/ppermute | solution.py:16
  472.2 1.3 copy-start.3
  513.6 16.7 %collective-permute-start.6 = (f32[1024,128]{0,1:T(8,128)S(1)}, f32[1024,128]{0,1:T(8,128)S(1)}, u32[]{:S(2)}, u32[]{:S(2)}) collective-permute-start(f32[1024,128]{0,1:T(8,128)S(1)} %get-tuple-element.5), channel_id=1, source_target_pairs={{0,8},{8,16},{16,24},{24,32},{32,40},{40,48},{48,56},{56,64},{64,7... | collective-permute-start | bytes 1572872 | tf_op jit(solution)/shard_map/ppermute | solution.py:16
  518.3 17.4 %collective-permute-start.7 = (f32[1024,128]{0,1:T(8,128)S(1)}, f32[1024,128]{0,1:T(8,128)S(1)}, u32[]{:S(2)}, u32[]{:S(2)}) collective-permute-start(f32[1024,128]{0,1:T(8,128)S(1)} %get-tuple-element.6), channel_id=1, source_target_pairs={{8,0},{16,8},{24,16},{32,24},{40,32},{48,40},{56,48},{64,56},{72,6... | collective-permute-start | bytes 1572872 | tf_op jit(solution)/shard_map/ppermute | solution.py:16
  535.8 1.4 copy-start.1
Sparse Core Ops, SparseCore 0:
  10.4 64.3 all-reduce.4
  143.8 61.4 all-reduce.6
  282.1 61.4 all-reduce.8
  409.9 61.4 all-reduce.10
where the time goes:
time: 555 us; the launch traced here: 544 us
  waiting for transfers between devices  307 us (55%)
  local copies, waits for them, and re-layouts  158 us (28%)
  starting transfers between devices  26.5 us (5%)
  between operations  20 us (4%)
  other arithmetic  19.6 us (4%)
  matrix products  13 us (2%)
    psum x4, waiting for transfers between devices, full_gram(): return lax.psum(inner_rows(paired, paired), 'row')  245 us
    gather x32, local copies, waits for them, and re-layouts, turn_pair(): diagonal_now = jnp.diagonal(gram)  86.4 us
    ppermute x8, waiting for transfers between devices, passed_along(): return lax.ppermute(array, axis, pairs)  61.8 us
    gather x32, local copies, waits for them, and re-layouts, turn_pair(): cross = jnp.diagonal(gram[:width, width:])  39.8 us
    ppermute x8, starting transfers between devices, passed_along(): return lax.ppermute(array, axis, pairs)  26.4 us
  transfers between devices with their start and end apart: 12, of which 12 were waited for; matrix products, arithmetic and copies ran while one was open for 0% of the time, Pallas kernels for 0%

commit v1 on v0

v1 whole, which is shorter than its diff:
```python
import jax
import jax.numpy as jnp
from jax import lax
from jax.experimental import pallas as pl
from jax.experimental.pallas import tpu as pltpu
from jax.sharding import PartitionSpec as P

ROUNDS = 4
STEPS = 8
W = 128
CHUNKS = 4
HIGH = lax.Precision.HIGHEST
MESH = pl.DeviceIdType.MESH
F32 = jnp.float32


def nt(a, b):
    return lax.dot_general(a, b, (((1,), (1,)), ((), ())), precision=HIGH, preferred_element_type=F32)


def tn(a, b):
    return lax.dot_general(a, b, (((0,), (0,)), ((), ())), precision=HIGH, preferred_element_type=F32)


def rotate_step(src, dst):
    row = lax.broadcasted_iota(jnp.int32, (W, W), 0)
    col = lax.broadcasted_iota(jnp.int32, (W, W), 1)
    eye = row == col
    lane = lax.broadcasted_iota(jnp.int32, (8, W), 1)

    def diag(k):
        return jnp.sum(jnp.where(eye, src[k, 8 : 8 + W], 0.0), axis=0, keepdims=True)

    a, g, b = diag(0), diag(1), diag(3)
    differ = b - a
    sign = jnp.where(differ >= 0, 1.0, -1.0)
    tangent = 2.0 * g * sign / (jnp.abs(differ) + jnp.sqrt(differ * differ + 4.0 * g * g) + 1e-06 * (a + b))
    cos = 1.0 / jnp.sqrt(1.0 + tangent * tangent)
    sin = cos * tangent
    cos_t = jnp.broadcast_to(cos, (W, W)).T
    sin_t = jnp.broadcast_to(sin, (W, W)).T
    c8 = jnp.broadcast_to(cos, (8, W))
    s8 = jnp.broadcast_to(sin, (8, W))

    def reorder(left, right):
        mixed = pltpu.roll(jnp.where(lane == 0, right, left), 1, 1)
        new_left = jnp.where(lane == 0, left, mixed)
        new_right = jnp.where(lane == W - 1, left, pltpu.roll(right, W - 1, 1))
        return new_left, new_right

    def put(k, i, top, bottom):
        lo = 8 * i
        dst[k, 9 + lo : 17 + lo] = top
        dst[k + 2, 7 + lo : 15 + lo] = bottom

    def ends(k, t0, b0, t127):
        dst[k, 8:9] = t0
        dst[k, 9:10] = b0
        dst[k + 2, 7 + W : 8 + W] = t127

    first = None
    for i in range(W // 8):
        at = slice(8 + 8 * i, 16 + 8 * i)
        ct, st = cos_t[8 * i : 8 * i + 8], sin_t[8 * i : 8 * i + 8]
        A, B, C, D = src[0, at], src[1, at], src[2, at], src[3, at]
        A1, B1 = A * c8 - B * s8, A * s8 + B * c8
        C1, D1 = C * c8 - D * s8, C * s8 + D * c8
        A2, C2 = ct * A1 - st * C1, st * A1 + ct * C1
        B2, D2 = ct * B1 - st * D1, st * B1 + ct * D1
        A3, B3 = reorder(A2, B2)
        C3, D3 = reorder(C2, D2)
        put(0, i, A3, C3)
        put(1, i, B3, D3)
        wtl, wtr, wbl, wbr = src[4, at], src[5, at], src[6, at], src[7, at]
        ntl, nbl = ct * wtl - st * wbl, st * wtl + ct * wbl
        ntr, nbr = ct * wtr - st * wbr, st * wtr + ct * wbr
        put(4, i, ntl, nbl)
        put(5, i, ntr, nbr)
        if i == 0:
            first = [(v[0:1], u[0:1]) for v, u in ((A3, C3), (B3, D3), (ntl, nbl), (ntr, nbr))]
    last = [v[7:8] for v in (A3, B3, ntl, ntr)]
    for k, (t0, b0), t127 in zip((0, 1, 4, 5), first, last):
        ends(k, t0, b0, t127)


def kernel(m_ref, flips_ref, out_top, out_bot, top, bot, xs, ys, state, part0, rs0, red0, sum0,
           part, rs, red, cross, gx, gy, gd, in_sem, mx_s, mt_r, my_s, mb_r, gx_s, gt_r, gy_s, gb_r,
           ag_s, ag_r, rs_s, rs_r, bc_s, bc_r):
    p = lax.axis_index("col")
    q = lax.axis_index("row")
    last = lax.axis_size("col") - 1
    n = lax.axis_size("row")
    rows = m_ref.shape[0]
    step = rows // CHUNKS

    loads = []
    for c in range(CHUNKS):
        at = pl.ds(c * step, step)
        for h, buf in enumerate((top, bot)):
            load = pltpu.make_async_copy(m_ref.at[at, pl.ds(h * W, W)], buf.at[0, at], in_sem.at[c, h])
            load.start()
            loads.append(load)

    barrier = pltpu.get_barrier_semaphore()
    for d in range(1, n):
        pl.semaphore_signal(barrier, inc=1, device_id={"row": lax.rem(q + d, n)}, device_id_type=MESH)

    @pl.when(p < last)
    def _():
        pl.semaphore_signal(barrier, inc=1, device_id={"col": p + 1}, device_id_type=MESH)

    @pl.when(p > 0)
    def _():
        pl.semaphore_signal(barrier, inc=1, device_id={"col": p - 1}, device_id_type=MESH)

    def remote(src, dst, s, r, where):
        return pltpu.make_async_remote_copy(
            src_ref=src, dst_ref=dst, send_sem=s, recv_sem=r, device_id=where, device_id_type=MESH)

    def all_reduce(r, size, part, rs, red, out):
        for d in range(1, n):
            t = lax.rem(q + d, n)
            remote(part.at[pl.ds(t * size, size)], rs.at[q], rs_s.at[r, d], rs_r.at[r, d], {"row": t}).start()
        rs[q] = part[pl.ds(pl.multiple_of(q * size, 16), size), :]
        for d in range(1, n):
            t = lax.rem(q + d, n)
            remote(part.at[pl.ds(t * size, size)], rs.at[q], rs_s.at[r, d], rs_r.at[r, d], {"row": t}).wait_recv()
        total = rs[0]
        for j in range(1, n):
            total = total + rs[j]
        red[...] = total
        mine = pl.ds(pl.multiple_of(q * size, 16), size)
        for d in range(1, n):
            t = lax.rem(q + d, n)
            remote(red, out.at[mine], bc_s.at[r, d], bc_r.at[r, d], {"row": t}).start()
        out[mine, :] = total
        for d in range(1, n):
            t = lax.rem(q + d, n)
            remote(red, out.at[mine], bc_s.at[r, d], bc_r.at[r, d], {"row": t}).wait()
            remote(part.at[pl.ds(t * size, size)], rs.at[q], rs_s.at[r, d], rs_r.at[r, d], {"row": t}).wait_send()

    g_tt = g_tb = g_bb = None
    for c in range(CHUNKS):
        loads[2 * c].wait()
        loads[2 * c + 1].wait()
        t = top[0, c * step : (c + 1) * step]
        b = bot[0, c * step : (c + 1) * step]
        tt, tb, bb = tn(t, t), tn(t, b), tn(b, b)
        g_tt = tt if c == 0 else g_tt + tt
        g_tb = tb if c == 0 else g_tb + tb
        g_bb = bb if c == 0 else g_bb + bb
    part0[0:W] = g_tt
    part0[W : 2 * W] = g_tb
    part0[2 * W : 3 * W] = g_bb

    met = n - 1 + (p > 0).astype(jnp.int32) + (p < last).astype(jnp.int32)
    pl.semaphore_wait(barrier, met)

    all_reduce(0, 3 * W // n, part0, rs0, red0, sum0)

    row = lax.broadcasted_iota(jnp.int32, (W, W), 0)
    col = lax.broadcasted_iota(jnp.int32, (W, W), 1)
    eye = jnp.where(row == col, 1.0, 0.0)
    zero = jnp.zeros((W, W), F32)

    for r in range(ROUNDS):
        inner = slice(8, 8 + W)
        if r == 0:
            g_tt, g_tb, g_bb = sum0[0:W], sum0[W : 2 * W], sum0[2 * W : 3 * W]
        else:
            g_tt = gd[r - 1, :, 0].reshape(W, W)
            g_bb = gd[r - 1, :, 1].reshape(W, W)
            g_tb = cross[r - 1]
        state[0, 0, inner] = g_tt
        state[0, 1, inner] = g_tb
        state[0, 2, inner] = g_tb.T
        state[0, 3, inner] = g_bb
        state[0, 4, inner] = eye
        state[0, 5, inner] = zero
        state[0, 6, inner] = zero
        state[0, 7, inner] = eye

        def two(_, carry):
            rotate_step(state.at[0], state.at[1])
            rotate_step(state.at[1], state.at[0])
            return carry

        lax.fori_loop(0, STEPS // 2, two, 0)

        flag = jnp.broadcast_to(flips_ref[r : r + 1, :], (W, W))
        swap = jnp.logical_xor(flag == 1, jnp.broadcast_to(p, (W, W)) == 0)

        def pick(k, j):
            u, v = state[0, k, inner], state[0, j, inner]
            return jnp.where(swap, v, u), jnp.where(swap, u, v)

        xl, yl = pick(4, 6)
        xr, yr = pick(5, 7)

        if r < ROUNDS - 1:
            gx[r], gy[r] = pick(0, 3)
            piece = pl.ds(pl.multiple_of(q * (W // n), 16), W // n)

            def send_gx():
                return remote(gx.at[r, piece], gd.at[r, q, 0], gx_s.at[r], gt_r.at[r], {"col": p + 1})

            def send_gy():
                return remote(gy.at[r, piece], gd.at[r, q, 1], gy_s.at[r], gb_r.at[r], {"col": p - 1})

            def keep_gx():
                return pltpu.make_async_copy(gx.at[r, piece], gd.at[r, q, 1], gb_r.at[r])

            def keep_gy():
                return pltpu.make_async_copy(gy.at[r, piece], gd.at[r, q, 0], gt_r.at[r])

            pl.when(p < last)(lambda: send_gx().start())
            pl.when(p == last)(lambda: keep_gx().start())
            pl.when(p > 0)(lambda: send_gy().start())
            pl.when(p == 0)(lambda: keep_gy().start())

        def dests(r, at):
            if r < ROUNDS - 1:
                return top.at[r + 1, at], bot.at[r + 1, at]
            return out_top.at[at], out_bot.at[at]

        def moves(r, c):
            at = pl.ds(c * step, step)
            to_top, to_bot = dests(r, at)
            right = lambda: remote(xs.at[r, at], to_top, mx_s.at[r, c], mt_r.at[r, c], {"col": p + 1})
            left = lambda: remote(ys.at[r, at], to_bot, my_s.at[r, c], mb_r.at[r, c], {"col": p - 1})
            keep_x = lambda: pltpu.make_async_copy(xs.at[r, at], to_bot, mb_r.at[r, c])
            keep_y = lambda: pltpu.make_async_copy(ys.at[r, at], to_top, mt_r.at[r, c])
            return right, left, keep_x, keep_y

        for c in range(CHUNKS):
            at = slice(c * step, (c + 1) * step)
            right, left, keep_x, keep_y = moves(r, c)
            t, b = top[r, at], bot[r, at]
            xs[r, at] = nt(t, xl) + nt(b, xr)
            pl.when(p < last)(lambda: right().start())
            pl.when(p == last)(lambda: keep_x().start())
            ys[r, at] = nt(t, yl) + nt(b, yr)
            pl.when(p > 0)(lambda: left().start())
            pl.when(p == 0)(lambda: keep_y().start())

        def arrived(c):
            right, left, keep_x, keep_y = moves(r, c)
            keep_y().wait()
            keep_x().wait()

        def sent():
            for c in range(CHUNKS):
                right, left, keep_x, keep_y = moves(r, c)
                pl.when(p < last)(lambda: right().wait_send())
                pl.when(p > 0)(lambda: left().wait_send())

        if r < ROUNDS - 1:
            keep_gy().wait()
            keep_gx().wait()

            def hand(d):
                t = lax.rem(q + d, n)
                return remote(gd.at[r, q], gd.at[r, q], ag_s.at[r, d], ag_r.at[r, d], {"row": t})

            for d in range(1, n):
                hand(d).start()

            total = None
            for c in range(CHUNKS):
                arrived(c)
                at = slice(c * step, (c + 1) * step)
                now = tn(top[r + 1, at], bot[r + 1, at])
                total = now if c == 0 else total + now
            part[r] = total
            all_reduce(r + 1, W // n, part.at[r], rs.at[r], red.at[r], cross.at[r])
            for d in range(1, n):
                hand(d).wait()
            pl.when(p < last)(lambda: send_gx().wait_send())
            pl.when(p > 0)(lambda: send_gy().wait_send())
            sent()
        else:
            for c in range(CHUNKS):
                arrived(c)
            sent()


def body(matrix, flips):
    rows = matrix.shape[0]
    n = lax.axis_size("row")
    R = ROUNDS
    dma = pltpu.SemaphoreType.DMA
    half = jax.ShapeDtypeStruct((rows, W), F32)
    top, bottom = pl.pallas_call(
        kernel,
        out_shape=(half, half),
        in_specs=[pl.BlockSpec(memory_space=pl.ANY), pl.BlockSpec(memory_space=pltpu.VMEM)],
        out_specs=(pl.BlockSpec(memory_space=pl.ANY), pl.BlockSpec(memory_space=pl.ANY)),
        scratch_shapes=[
            pltpu.VMEM((R, rows, W), F32),
            pltpu.VMEM((R, rows, W), F32),
            pltpu.VMEM((R, rows, W), F32),
            pltpu.VMEM((R, rows, W), F32),
            pltpu.VMEM((2, 8, W + 16, W), F32),
            pltpu.VMEM((3 * W, W), F32),
            pltpu.VMEM((n, 3 * W // n, W), F32),
            pltpu.VMEM((3 * W // n, W), F32),
            pltpu.VMEM((3 * W, W), F32),
            pltpu.VMEM((R - 1, W, W), F32),
            pltpu.VMEM((R - 1, n, W // n, W), F32),
            pltpu.VMEM((R - 1, W // n, W), F32),
            pltpu.VMEM((R - 1, W, W), F32),
            pltpu.VMEM((R - 1, W, W), F32),
            pltpu.VMEM((R - 1, W, W), F32),
            pltpu.VMEM((R - 1, n, 2, W // n, W), F32),
            dma((CHUNKS, 2)),
            dma((R, CHUNKS)),
            dma((R, CHUNKS)),
            dma((R, CHUNKS)),
            dma((R, CHUNKS)),
            dma((R,)),
            dma((R,)),
            dma((R,)),
            dma((R,)),
            dma((R, n)),
            dma((R, n)),
            dma((R, n)),
            dma((R, n)),
            dma((R, n)),
            dma((R, n)),
        ],
        compiler_params=pltpu.CompilerParams(
            collective_id=0, has_side_effects=True, vmem_limit_bytes=40 * 1024 * 1024),
    )(matrix, flips)
    return jnp.concatenate([top, bottom], axis=1)


def solution(mesh):
    placed = (P("row", "col"), P(None, "col"))
    return jax.shard_map(
        body, mesh=mesh, in_specs=placed, out_specs=P("row", "col"), check_vma=False
    )
```

time: 555 us -> 114 us (0.21)
  the two profiles are of different devices: /device:TPU:120 before, /device:TPU:7 now
where the time goes in v1:
time: 114 us
  Pallas kernels  111 us (97%)
  local copies, waits for them, and re-layouts  1.96 us (2%)
    pallas_call x1, Pallas kernels, body(): pl.pallas_call(kernel, out_shape=(half, half), in_specs=[pl.BlockSpec(mem...  111 us

profile of v1, /device:TPU:7, one launch (start us, length us, event | category | flops | bytes accessed | tf_op | source)
XLA Modules:
  0.0 113.9 jit_solution(9324461710948310846)
XLA Ops:
  0.0 0.7 copy.3.flips_ref
  0.7 0.0 copy-start
  0.7 1.2 %copy-done = f32[1024,256]{1,0:T(8,128)S(1)} copy-done((f32[1024,256]{1,0:T(8,128)S(1)}, f32[1024,256]{1,0:T(8,128)}, u32[]{:S(2)}) %copy-start) | copy-done | bytes 1048600
  2.0 110.9 %shard_map.28 = (f32[1024,128]{1,0:T(8,128)S(1)}, f32[1024,128]{1,0:T(8,128)S(1)}) custom-call(f32[1024,256]{1,0:T(8,128)S(1)} %copy-done, s32[4,1]{1,0:T(4,128)S(1)} %copy.3.flips_ref), custom_call_target="tpu_custom_call" | custom-call | tf_op jit(solution)/shard_map/pallas_call | solution.py:293
  112.8 1.0 pad_maximum_fusion
Async XLA Ops:
  0.7 1.2 %copy-start = (f32[1024,256]{1,0:T(8,128)S(1)}, f32[1024,256]{1,0:T(8,128)}, u32[]{:S(2)}) copy-start(f32[1024,256]{1,0:T(8,128)} %m_ref.1) | copy-start | bytes 3145732

commit v2 on v0

v2 whole, which is shorter than its diff:
```python
import jax
import jax.numpy as jnp
from jax import lax
from jax.experimental import pallas as pl
from jax.experimental.pallas import tpu as pltpu
from jax.sharding import PartitionSpec as P

ROUNDS = 4
STEPS = 8
W = 128
H = W // 2
PAD = 8
CHUNKS = 4
RAW = 2
MESH = pl.DeviceIdType.MESH
F32 = jnp.float32
BF16 = jnp.bfloat16
INNER = slice(PAD, PAD + W)


def dot(a, b, ca, cb):
    return lax.dot_general(a, b, (((ca,), (cb,)), ((), ())), preferred_element_type=F32)


def split(x):
    high = x.astype(BF16)
    return high, (x - high.astype(F32)).astype(BF16)


def full_gram(m):
    high, low = split(m)
    cross = dot(high, low, 0, 0)
    return dot(high, high, 0, 0) + (cross + cross.T)


def cross_gram(t, b):
    four = dot(jnp.concatenate(split(t), axis=1), jnp.concatenate(split(b), axis=1), 0, 0)
    return four[:W, :W] + (four[:W, W:] + four[W:, :W] + four[W:, W:])


def times(t, b, turn):
    high, low = split(jnp.concatenate([t, b], axis=1))
    return dot(high, turn[0], 1, 1) + (dot(high, turn[1], 1, 1) + dot(low, turn[0], 1, 1))


def cos_sin(tangent):
    cos = lax.rsqrt(1.0 + tangent * tangent)
    return cos, cos * tangent


def down(v):
    return jnp.broadcast_to(v, (W, W)).T


def put(dst, k, i, top, bottom):
    lo = PAD + 8 * i
    dst[k, lo + 1 : lo + 9] = top
    dst[k + 2, lo - 1 : lo + 7] = bottom


def put_ends(dst, k, first_top, first_bottom, last_top):
    dst[k, PAD : PAD + 1] = first_top[0:1]
    dst[k, PAD + 1 : PAD + 2] = first_bottom[0:1]
    dst[k + 2, PAD + W - 1 : PAD + W] = last_top[7:8]


def gram_step(src, dst):
    row = lax.broadcasted_iota(jnp.int32, (W, W), 0)
    col = lax.broadcasted_iota(jnp.int32, (W, W), 1)
    eye = row == col
    lane = lax.broadcasted_iota(jnp.int32, (8, W), 1)

    def diag(k):
        return jnp.sum(jnp.where(eye, src[k, INNER], 0.0), axis=0, keepdims=True)

    a, g, b = diag(0), diag(1), diag(3)
    differ = b - a
    sign = jnp.where(differ >= 0, 1.0, -1.0)
    tangent = 2.0 * g * sign / (jnp.abs(differ) + jnp.sqrt(differ * differ + 4.0 * g * g) + 1e-06 * (a + b))
    cos, sin = cos_sin(tangent)
    cos_t, sin_t = down(cos), down(sin)
    c8 = jnp.broadcast_to(cos, (8, W))
    s8 = jnp.broadcast_to(sin, (8, W))

    def reorder(left, right):
        mixed = pltpu.roll(jnp.where(lane == 0, right, left), 1, 1)
        new_left = jnp.where(lane == 0, left, mixed)
        new_right = jnp.where(lane == W - 1, left, pltpu.roll(right, W - 1, 1))
        return new_left, new_right

    first = None
    for i in range(W // 8):
        at = slice(PAD + 8 * i, PAD + 8 * i + 8)
        ct, st = cos_t[8 * i : 8 * i + 8], sin_t[8 * i : 8 * i + 8]
        A, B, C, D = src[0, at], src[1, at], src[2, at], src[3, at]
        A1, B1 = A * c8 - B * s8, A * s8 + B * c8
        C1, D1 = C * c8 - D * s8, C * s8 + D * c8
        A2, C2 = ct * A1 - st * C1, st * A1 + ct * C1
        B2, D2 = ct * B1 - st * D1, st * B1 + ct * D1
        A3, B3 = reorder(A2, B2)
        C3, D3 = reorder(C2, D2)
        put(dst, 0, i, A3, C3)
        put(dst, 1, i, B3, D3)
        if i == 0:
            first = (A3, C3, B3, D3)
    put_ends(dst, 0, first[0], first[1], A3)
    put_ends(dst, 1, first[2], first[3], B3)
    return tangent


def basis_step(src, dst, tangent):
    cos, sin = cos_sin(tangent)
    cos_t, sin_t = down(cos), down(sin)
    first = None
    for i in range(W // 8):
        at = slice(PAD + 8 * i, PAD + 8 * i + 8)
        ct, st = cos_t[8 * i : 8 * i + 8], sin_t[8 * i : 8 * i + 8]
        tl, tr, bl, br = src[0, at], src[1, at], src[2, at], src[3, at]
        ntl, nbl = ct * tl - st * bl, st * tl + ct * bl
        ntr, nbr = ct * tr - st * br, st * tr + ct * br
        put(dst, 0, i, ntl, nbl)
        put(dst, 1, i, ntr, nbr)
        if i == 0:
            first = (ntl, nbl, ntr, nbr)
    put_ends(dst, 0, first[0], first[1], ntl)
    put_ends(dst, 1, first[2], first[3], ntr)


def rebuild(messages, bases):
    row = lax.broadcasted_iota(jnp.int32, (W, W), 0)
    col = lax.broadcasted_iota(jnp.int32, (W, W), 1)
    eye = jnp.where(row == col, 1.0, 0.0)
    zero = jnp.zeros((W, W), F32)
    for base in bases:
        for k, value in enumerate((eye, zero, zero, eye)):
            base[0, k, INNER] = value

    def two(i, carry):
        for half in range(2):
            for message, base in zip(messages, bases):
                basis_step(base.at[half], base.at[1 - half], message[pl.ds(2 * i + half, 1), :])
        return carry

    lax.fori_loop(0, STEPS // 2, two, 0)


def halves(message, base):
    swap = jnp.broadcast_to(message[STEPS : STEPS + 1, :], (W, W)) > 0.5
    tl, tr, bl, br = (base[0, k, INNER] for k in range(4))
    right = jnp.concatenate([jnp.where(swap, bl, tl), jnp.where(swap, br, tr)], axis=1)
    left = jnp.concatenate([jnp.where(swap, tl, bl), jnp.where(swap, tr, br)], axis=1)
    return right, left


def kernel(m_ref, flips_ref, out_top, out_bot, top, bot, xs, ys, ft, fb, lb, rt, gram, base, base_l, base_r,
           part0, sib0, slabs0, sum0, part, sib, slabs, cross, msg, lmsg, rmsg, gx, gy, gt, gb,
           in_sem, ft_s, ft_r, fb_s, fb_r, lb_s, lb_r, rt_s, rt_r, x_s, x_r, y_s, y_r,
           ml_s, ml_r, mr_s, mr_r, gx_s, gt_r, gy_s, gb_r, one_s, one_r, far0_s, far0_r, sib_s, sib_r, far_s, far_r):
    p = lax.axis_index("col")
    q = lax.axis_index("row")
    last = lax.axis_size("col") - 1
    n = lax.axis_size("row")
    rows = m_ref.shape[0]
    step = rows // CHUNKS
    core = lax.rem(q, 2)
    chip = q // 2
    sibling = {"row": q + 1 - 2 * core}
    right = {"col": p + 1}
    left = {"col": p - 1}
    finish = []

    def others(d):
        return {"row": lax.rem(q + 2 * d, n)}

    def part_of(c):
        return pl.ds(c * step, step)

    def remote(src, dst, s, r, where):
        return pltpu.make_async_remote_copy(
            src_ref=src, dst_ref=dst, send_sem=s, recv_sem=r, device_id=where, device_id_type=MESH)

    def go_right(src, dst, s, r):
        pl.when(p < last)(lambda: remote(src, dst, s, r, right).start())
        finish.append(lambda: pl.when(p < last)(lambda: remote(src, dst, s, r, right).wait_send()))

    def go_left(src, dst, s, r):
        pl.when(p > 0)(lambda: remote(src, dst, s, r, left).start())
        finish.append(lambda: pl.when(p > 0)(lambda: remote(src, dst, s, r, left).wait_send()))

    def stay_first(src, dst, r):
        pl.when(p == 0)(lambda: pltpu.make_async_copy(src, dst, r).start())

    def stay_last(src, dst, r):
        pl.when(p == last)(lambda: pltpu.make_async_copy(src, dst, r).start())

    def arrived(dst, r):
        pltpu.make_async_copy(dst, dst, r).wait()

    loads = []
    for c in range(CHUNKS):
        at = part_of(c)
        for h, buf in enumerate((top, bot)):
            load = pltpu.make_async_copy(m_ref.at[at, pl.ds(h * W, W)], buf.at[0, at], in_sem.at[c, h])
            load.start()
            loads.append(load)

    barrier = pltpu.get_barrier_semaphore()
    for where in [sibling] + [others(d) for d in range(1, n // 2)]:
        pl.semaphore_signal(barrier, inc=1, device_id=where, device_id_type=MESH)

    @pl.when(p < last)
    def _():
        pl.semaphore_signal(barrier, inc=1, device_id=right, device_id_type=MESH)

    @pl.when(p > 0)
    def _():
        pl.semaphore_signal(barrier, inc=1, device_id=left, device_id_type=MESH)

    def sum_first():
        near = remote(part0.at[1 - core], sib0, one_s.at[0], one_r.at[0], sibling)
        near.start()
        near.wait_recv()
        slabs0[chip] = part0[core] + sib0[...]
        far = [
            remote(slabs0.at[chip], slabs0.at[chip], far0_s.at[d], far0_r.at[d], others(d))
            for d in range(1, n // 2)
        ]
        for copy in far:
            copy.start()
        for copy in far:
            copy.wait_recv()
        total = slabs0[0]
        for j in range(1, n // 2):
            total = total + slabs0[j]
        sum0[core] = total
        back = remote(sum0.at[core], sum0.at[core], one_s.at[1], one_r.at[1], sibling)
        back.start()
        back.wait_recv()
        for copy in [near, back] + far:
            finish.append(copy.wait_send)

    def sum_small(r):
        near = remote(part.at[r], sib.at[r], sib_s.at[r], sib_r.at[r], sibling)
        near.start()
        near.wait_recv()
        slabs[r, chip] = part[r] + sib[r]
        far = [
            remote(slabs.at[r, chip], slabs.at[r, chip], far_s.at[r, d], far_r.at[r, d], others(d))
            for d in range(1, n // 2)
        ]
        for copy in far:
            copy.start()
        for copy in far:
            copy.wait_recv()
        total = slabs[r, 0]
        for j in range(1, n // 2):
            total = total + slabs[r, j]
        cross[r] = total
        for copy in [near] + far:
            finish.append(copy.wait_send)

    total = None
    for c in range(CHUNKS):
        loads[2 * c].wait()
        loads[2 * c + 1].wait()
        at = slice(c * step, (c + 1) * step)
        now = full_gram(jnp.concatenate([top[0, at], bot[0, at]], axis=1))
        total = now if c == 0 else total + now
    part0[0, 0:W] = total[:W, :W]
    part0[0, W:] = total[:H, W:]
    part0[1, 0:H] = total[H:W, W:]
    part0[1, H:] = total[W:, W:]

    met = n // 2 + (p > 0).astype(jnp.int32) + (p < last).astype(jnp.int32)
    pl.semaphore_wait(barrier, met)

    def forward(r, c):
        at = part_of(c)
        go_right(top.at[r, at], ft.at[r, at], ft_s.at[r, c], ft_r.at[r, c])
        go_left(bot.at[r, at], fb.at[r, at], fb_s.at[r, c], fb_r.at[r, c])
        stay_first(top.at[r, at], ft.at[r, at], ft_r.at[r, c])
        stay_last(bot.at[r, at], fb.at[r, at], fb_r.at[r, c])

    for c in range(RAW):
        at = part_of(c)
        forward(0, c)
        go_right(bot.at[0, at], lb.at[at], lb_s.at[c], lb_r.at[c])
        go_left(top.at[0, at], rt.at[at], rt_s.at[c], rt_r.at[c])
        stay_first(bot.at[0, at], lb.at[at], lb_r.at[c])
        stay_last(top.at[0, at], rt.at[at], rt_r.at[c])

    sum_first()

    for r in range(ROUNDS):
        if r == 0:
            g_tt, g_bb = sum0[0, 0:W], sum0[1, H:]
            g_tb = jnp.concatenate([sum0[0, W:], sum0[1, 0:H]], axis=0)
        else:
            arrived(gt.at[r - 1], gt_r.at[r - 1])
            arrived(gb.at[r - 1], gb_r.at[r - 1])
            g_tt, g_bb, g_tb = gt[r - 1], gb[r - 1], cross[r - 1]
        for k, value in enumerate((g_tt, g_tb, g_tb.T, g_bb)):
            gram[0, k, INNER] = value

        def two(i, carry):
            msg[r, pl.ds(2 * i, 1)] = gram_step(gram.at[0], gram.at[1])
            msg[r, pl.ds(2 * i + 1, 1)] = gram_step(gram.at[1], gram.at[0])
            return carry

        lax.fori_loop(0, STEPS // 2, two, 0)
        flag = jnp.broadcast_to(flips_ref[:, r : r + 1], (8, W)) == 1
        swap = jnp.logical_xor(flag, jnp.broadcast_to(p, (8, W)) == 0)
        msg[r, STEPS:] = jnp.where(swap, 1.0, 0.0)
        go_right(msg.at[r], lmsg.at[r], ml_s.at[r], ml_r.at[r])
        go_left(msg.at[r], rmsg.at[r], mr_s.at[r], mr_r.at[r])
        stay_first(msg.at[r], lmsg.at[r], ml_r.at[r])
        stay_last(msg.at[r], rmsg.at[r], mr_r.at[r])

        if r < ROUNDS - 1:
            swaps = jnp.broadcast_to(msg[r, STEPS : STEPS + 1], (W, W)) > 0.5
            u, v = gram[0, 0, INNER], gram[0, 3, INNER]
            gx[r] = jnp.where(swaps, v, u)
            gy[r] = jnp.where(swaps, u, v)
            go_right(gx.at[r], gt.at[r], gx_s.at[r], gt_r.at[r])
            go_left(gy.at[r], gb.at[r], gy_s.at[r], gb_r.at[r])
            stay_last(gx.at[r], gb.at[r], gb_r.at[r])
            stay_first(gy.at[r], gt.at[r], gt_r.at[r])

        rebuild([msg.at[r]], [base])
        turn = split(jnp.concatenate(halves(msg.at[r], base), axis=0))
        for c in [*range(RAW, CHUNKS), *range(RAW)]:
            at = slice(c * step, (c + 1) * step)
            new = times(top[r, at], bot[r, at], turn)
            xs[r, at] = new[:, :W]
            ys[r, at] = new[:, W:]
            if r == 0 and c >= RAW:
                src = part_of(c)
                go_right(xs.at[r, src], top.at[1, src], x_s.at[c], x_r.at[c])
                go_left(ys.at[r, src], bot.at[1, src], y_s.at[c], y_r.at[c])
                stay_first(ys.at[r, src], top.at[1, src], x_r.at[c])
                stay_last(xs.at[r, src], bot.at[1, src], y_r.at[c])

        arrived(lmsg.at[r], ml_r.at[r])
        arrived(rmsg.at[r], mr_r.at[r])
        rebuild([lmsg.at[r], rmsg.at[r]], [base_l, base_r])
        turn_l = split(halves(lmsg.at[r], base_l)[0])
        turn_r = split(halves(rmsg.at[r], base_r)[1])
        at_first = jnp.broadcast_to(p, (step, W)) == 0
        at_last = jnp.broadcast_to(p, (step, W)) == last
        total = None
        for c in range(CHUNKS):
            at = slice(c * step, (c + 1) * step)
            ref = part_of(c)
            if r == 0 and c >= RAW:
                arrived(top.at[1, ref], x_r.at[c])
                arrived(bot.at[1, ref], y_r.at[c])
                new_top, new_bot = top[1, at], bot[1, at]
            else:
                arrived(ft.at[r, ref], ft_r.at[r, c])
                arrived(fb.at[r, ref], fb_r.at[r, c])
                if r == 0:
                    arrived(lb.at[ref], lb_r.at[c])
                    arrived(rt.at[ref], rt_r.at[c])
                    l_b, r_t = lb[at], rt[at]
                else:
                    l_b, r_t = ys[r - 1, at], xs[r - 1, at]
                new_top = jnp.where(at_first, ys[r, at], times(ft[r, at], l_b, turn_l))
                new_bot = jnp.where(at_last, xs[r, at], times(r_t, fb[r, at], turn_r))
                if r < ROUNDS - 1:
                    top[r + 1, at] = new_top
                    bot[r + 1, at] = new_bot
                else:
                    out_top[at] = new_top
                    out_bot[at] = new_bot
            if r < ROUNDS - 1:
                forward(r + 1, c)
                now = cross_gram(new_top, new_bot)
                total = now if c == 0 else total + now
        if r < ROUNDS - 1:
            part[r] = total
            sum_small(r)

    for wait in finish:
        wait()


def body(matrix, flips):
    rows = matrix.shape[0]
    n = lax.axis_size("row")
    R = ROUNDS
    C = CHUNKS
    dma = pltpu.SemaphoreType.DMA
    half = jax.ShapeDtypeStruct((rows, W), F32)

    def vmem(*shape):
        return pltpu.VMEM(shape, F32)

    top, bottom = pl.pallas_call(
        kernel,
        out_shape=(half, half),
        in_specs=[pl.BlockSpec(memory_space=pl.ANY), pl.BlockSpec(memory_space=pltpu.VMEM)],
        out_specs=(pl.BlockSpec(memory_space=pltpu.VMEM), pl.BlockSpec(memory_space=pltpu.VMEM)),
        scratch_shapes=[
            *(vmem(R, rows, W) for _ in range(6)),
            *(vmem(rows, W) for _ in range(2)),
            *(vmem(2, 4, W + 2 * PAD, W) for _ in range(4)),
            vmem(2, W + H, W),
            vmem(W + H, W),
            vmem(n // 2, W + H, W),
            vmem(2, W + H, W),
            vmem(R - 1, W, W),
            vmem(R - 1, W, W),
            vmem(R - 1, n // 2, W, W),
            vmem(R - 1, W, W),
            *(vmem(R, 2 * STEPS, W) for _ in range(3)),
            *(vmem(R - 1, W, W) for _ in range(4)),
            dma((C, 2)),
            *(dma((R, C)) for _ in range(4)),
            *(dma((C,)) for _ in range(8)),
            *(dma((R,)) for _ in range(8)),
            dma((2,)),
            dma((2,)),
            dma((n // 2,)),
            dma((n // 2,)),
            dma((R,)),
            dma((R,)),
            dma((R, n // 2)),
            dma((R, n // 2)),
        ],
        compiler_params=pltpu.CompilerParams(
            collective_id=0, has_side_effects=True, vmem_limit_bytes=60 * 1024 * 1024),
    )(matrix, flips.T)
    return jnp.concatenate([top, bottom], axis=1)


def solution(mesh):
    placed = (P("row", "col"), P(None, "col"))
    return jax.shard_map(
        body, mesh=mesh, in_specs=placed, out_specs=P("row", "col"), check_vma=False
    )
```

time: 555 us -> 81.1 us (0.15)
  the two profiles are of different devices: /device:TPU:120 before, /device:TPU:7 now
where the time goes in v2:
time: 81.1 us; the launch traced here: 81 us
  Pallas kernels  78.7 us (97%)
  other arithmetic  2.24 us (3%)
    pallas_call x1, Pallas kernels, body(): pl.pallas_call(kernel, out_shape=(half, half), in_specs=[pl.BlockSpec(mem...  78.7 us
    concatenate x1, other arithmetic, body(): return jnp.concatenate([top, bottom], axis=1)  2.24 us

profile of v2, /device:TPU:7, one launch (start us, length us, event | category | flops | bytes accessed | tf_op | source)
XLA Modules:
  0.0 81.0 jit_solution(12873452365028913012)
XLA Ops:
  0.0 78.7 %shard_map.28 = (f32[1024,128]{1,0:T(8,128)}, f32[1024,128]{1,0:T(8,128)}) custom-call(f32[1024,256]{1,0:T(8,128)} %m_ref.1, s32[1,4]{1,0:T(1,128)} %bitcast.1), custom_call_target="tpu_custom_call" | custom-call | tf_op jit(solution)/shard_map/pallas_call | solution.py:398
  78.7 2.2 %pad_maximum_fusion = f32[1024,256]{1,0:T(8,128)} fusion(f32[1024,128]{1,0:T(8,128)} %get-tuple-element.8, f32[1024,128]{1,0:T(8,128)} %get-tuple-element.7), kind=kLoop, calls=%fused_computation | loop fusion | flops 262144 | bytes 2097152 | tf_op jit(solution)/shard_map/concatenate | solution.py:433

commit v3 on v2

--- a/solution.py
+++ b/solution.py
@@ -10,8 +10,10 @@
 W = 128
 H = W // 2
 PAD = 8
-CHUNKS = 4
+SIZES = (320, 320, 192, 192)
+CHUNKS = len(SIZES)
 RAW = 2
+PART = STEPS // 2
 MESH = pl.DeviceIdType.MESH
 F32 = jnp.float32
 BF16 = jnp.bfloat16
@@ -64,23 +66,28 @@
     dst[k + 2, PAD + W - 1 : PAD + W] = last_top[7:8]
 
 
-def gram_step(src, dst):
-    row = lax.broadcasted_iota(jnp.int32, (W, W), 0)
-    col = lax.broadcasted_iota(jnp.int32, (W, W), 1)
-    eye = row == col
+def pick_start(src):
+    row = lax.broadcasted_iota(jnp.int32, (8, W), 0)
     lane = lax.broadcasted_iota(jnp.int32, (8, W), 1)
-
-    def diag(k):
-        return jnp.sum(jnp.where(eye, src[k, INNER], 0.0), axis=0, keepdims=True)
-
-    a, g, b = diag(0), diag(1), diag(3)
+    sums = []
+    for k in (0, 1, 3):
+        total = None
+        for i in range(W // 8):
+            now = jnp.where(lane == row + 8 * i, src[k, PAD + 8 * i : PAD + 8 * i + 8], 0.0)
+            total = now if i == 0 else total + now
+        sums.append(jnp.broadcast_to(jnp.sum(total, axis=0, keepdims=True), (8, W)))
+    return tuple(sums)
+
+
+def gram_step(src, dst, picked):
+    row = lax.broadcasted_iota(jnp.int32, (8, W), 0)
+    lane = lax.broadcasted_iota(jnp.int32, (8, W), 1)
+    a, g, b = picked
     differ = b - a
     sign = jnp.where(differ >= 0, 1.0, -1.0)
     tangent = 2.0 * g * sign / (jnp.abs(differ) + jnp.sqrt(differ * differ + 4.0 * g * g) + 1e-06 * (a + b))
-    cos, sin = cos_sin(tangent)
-    cos_t, sin_t = down(cos), down(sin)
-    c8 = jnp.broadcast_to(cos, (8, W))
-    s8 = jnp.broadcast_to(sin, (8, W))
+    c8, s8 = cos_sin(tangent)
+    cos_t, sin_t = down(c8[0:1]), down(s8[0:1])
 
     def reorder(left, right):
         mixed = pltpu.roll(jnp.where(lane == 0, right, left), 1, 1)
@@ -88,7 +95,11 @@
         new_right = jnp.where(lane == W - 1, left, pltpu.roll(right, W - 1, 1))
         return new_left, new_right
 
-    first = None
+    def add(total, mask, value):
+        value = jnp.where(mask, value, 0.0)
+        return value if total is None else total + value
+
+    first = a_next = g_next = b_next = None
     for i in range(W // 8):
         at = slice(PAD + 8 * i, PAD + 8 * i + 8)
         ct, st = cos_t[8 * i : 8 * i + 8], sin_t[8 * i : 8 * i + 8]
@@ -101,11 +112,22 @@
         C3, D3 = reorder(C2, D2)
         put(dst, 0, i, A3, C3)
         put(dst, 1, i, B3, D3)
+        up = lane == row + (8 * i + 1)
         if i == 0:
             first = (A3, C3, B3, D3)
+            up = jnp.logical_or(jnp.logical_and(up, row > 0), jnp.logical_and(lane == 0, row == 0))
+            second = jnp.logical_and(lane == 1, row == 0)
+            a_next = add(a_next, second, C3)
+            g_next = add(g_next, second, D3)
+        a_next = add(a_next, up, A3)
+        g_next = add(g_next, up, B3)
+        b_next = add(b_next, lane == row + (8 * i - 1), D3)
+    b_next = add(b_next, jnp.logical_and(lane == W - 1, row == 7), B3)
     put_ends(dst, 0, first[0], first[1], A3)
     put_ends(dst, 1, first[2], first[3], B3)
-    return tangent
+    picked = tuple(
+        jnp.broadcast_to(jnp.sum(v, axis=0, keepdims=True), (8, W)) for v in (a_next, g_next, b_next))
+    return tangent[0:1], picked
 
 
 def basis_step(src, dst, tangent):
@@ -126,7 +148,7 @@
     put_ends(dst, 1, first[2], first[3], ntr)
 
 
-def rebuild(messages, bases):
+def identity(bases):
     row = lax.broadcasted_iota(jnp.int32, (W, W), 0)
     col = lax.broadcasted_iota(jnp.int32, (W, W), 1)
     eye = jnp.where(row == col, 1.0, 0.0)
@@ -135,33 +157,32 @@
         for k, value in enumerate((eye, zero, zero, eye)):
             base[0, k, INNER] = value
 
-    def two(i, carry):
-        for half in range(2):
-            for message, base in zip(messages, bases):
-                basis_step(base.at[half], base.at[1 - half], message[pl.ds(2 * i + half, 1), :])
-        return carry
-
-    lax.fori_loop(0, STEPS // 2, two, 0)
-
-
-def halves(message, base):
-    swap = jnp.broadcast_to(message[STEPS : STEPS + 1, :], (W, W)) > 0.5
+
+def rebuild(parts, bases):
+    for i in range(PART):
+        for part, base in zip(parts, bases):
+            basis_step(base.at[i % 2], base.at[1 - i % 2], part[i : i + 1, :])
+
+
+def halves(part, base):
+    swap = jnp.broadcast_to(part[PART : PART + 1, :], (W, W)) > 0.5
     tl, tr, bl, br = (base[0, k, INNER] for k in range(4))
     right = jnp.concatenate([jnp.where(swap, bl, tl), jnp.where(swap, br, tr)], axis=1)
     left = jnp.concatenate([jnp.where(swap, tl, bl), jnp.where(swap, tr, br)], axis=1)
     return right, left
 
 
-def kernel(m_ref, flips_ref, out_top, out_bot, top, bot, xs, ys, ft, fb, lb, rt, gram, base, base_l, base_r,
+def kernel(m_ref, flips_ref, out, done, top, bot, xs, ys, ft, fb, lb, rt, gram, base, base_l, base_r,
            part0, sib0, slabs0, sum0, part, sib, slabs, cross, msg, lmsg, rmsg, gx, gy, gt, gb,
-           in_sem, ft_s, ft_r, fb_s, fb_r, lb_s, lb_r, rt_s, rt_r, x_s, x_r, y_s, y_r,
+           in_sem, out_sem, ft_s, ft_r, fb_s, fb_r, lb_s, lb_r, rt_s, rt_r, x_s, x_r, y_s, y_r,
            ml_s, ml_r, mr_s, mr_r, gx_s, gt_r, gy_s, gb_r, one_s, one_r, far0_s, far0_r, sib_s, sib_r, far_s, far_r):
     p = lax.axis_index("col")
     q = lax.axis_index("row")
     last = lax.axis_size("col") - 1
     n = lax.axis_size("row")
     rows = m_ref.shape[0]
-    step = rows // CHUNKS
+    sizes = [size * rows // 1024 for size in SIZES]
+    begins = [sum(sizes[:c]) for c in range(CHUNKS)]
     core = lax.rem(q, 2)
     chip = q // 2
     sibling = {"row": q + 1 - 2 * core}
@@ -173,7 +194,10 @@
         return {"row": lax.rem(q + 2 * d, n)}
 
     def part_of(c):
-        return pl.ds(c * step, step)
+        return pl.ds(begins[c], sizes[c])
+
+    def rows_of(c):
+        return slice(begins[c], begins[c] + sizes[c])
 
     def remote(src, dst, s, r, where):
         return pltpu.make_async_remote_copy(
@@ -239,7 +263,7 @@
         for copy in [near, back] + far:
             finish.append(copy.wait_send)
 
-    def sum_small(r):
+    def sum_small(r, old):
         near = remote(part.at[r], sib.at[r], sib_s.at[r], sib_r.at[r], sibling)
         near.start()
         near.wait_recv()
@@ -250,6 +274,8 @@
         ]
         for copy in far:
             copy.start()
+        for wait in old:
+            wait()
         for copy in far:
             copy.wait_recv()
         total = slabs[r, 0]
@@ -263,13 +289,18 @@
     for c in range(CHUNKS):
         loads[2 * c].wait()
         loads[2 * c + 1].wait()
-        at = slice(c * step, (c + 1) * step)
+        at = rows_of(c)
         now = full_gram(jnp.concatenate([top[0, at], bot[0, at]], axis=1))
         total = now if c == 0 else total + now
-    part0[0, 0:W] = total[:W, :W]
-    part0[0, W:] = total[:H, W:]
-    part0[1, 0:H] = total[H:W, W:]
-    part0[1, H:] = total[W:, W:]
+    upper, lower = total[:W, :W], total[W:, W:]
+    row = lax.broadcasted_iota(jnp.int32, (W, W), 0)
+    col = lax.broadcasted_iota(jnp.int32, (W, W), 1)
+    both = jnp.where(row <= col, upper, lower)
+    ends = jnp.sum(jnp.where(row == col, lower, 0.0), axis=0, keepdims=True)
+    for h in range(2):
+        part0[h, 0:H] = both[h * H : (h + 1) * H]
+        part0[h, H:W] = total[h * H : (h + 1) * H, W:]
+        part0[h, W:] = jnp.broadcast_to(ends, (8, W))
 
     met = n // 2 + (p > 0).astype(jnp.int32) + (p < last).astype(jnp.int32)
     pl.semaphore_wait(barrier, met)
@@ -293,8 +324,12 @@
 
     for r in range(ROUNDS):
         if r == 0:
-            g_tt, g_bb = sum0[0, 0:W], sum0[1, H:]
-            g_tb = jnp.concatenate([sum0[0, W:], sum0[1, 0:H]], axis=0)
+            g_tb = jnp.concatenate([sum0[0, H:W], sum0[1, H:W]], axis=0)
+            both = jnp.concatenate([sum0[0, 0:H], sum0[1, 0:H]], axis=0)
+            both_t = both.T
+            ends = jnp.broadcast_to(sum0[0, W : W + 1], (W, W))
+            g_tt = jnp.where(row <= col, both, both_t)
+            g_bb = jnp.where(row > col, both, jnp.where(row < col, both_t, ends))
         else:
             arrived(gt.at[r - 1], gt_r.at[r - 1])
             arrived(gb.at[r - 1], gb_r.at[r - 1])
@@ -302,22 +337,29 @@
         for k, value in enumerate((g_tt, g_tb, g_tb.T, g_bb)):
             gram[0, k, INNER] = value
 
-        def two(i, carry):
-            msg[r, pl.ds(2 * i, 1)] = gram_step(gram.at[0], gram.at[1])
-            msg[r, pl.ds(2 * i + 1, 1)] = gram_step(gram.at[1], gram.at[0])
-            return carry
-
-        lax.fori_loop(0, STEPS // 2, two, 0)
         flag = jnp.broadcast_to(flips_ref[:, r : r + 1], (8, W)) == 1
         swap = jnp.logical_xor(flag, jnp.broadcast_to(p, (8, W)) == 0)
-        msg[r, STEPS:] = jnp.where(swap, 1.0, 0.0)
-        go_right(msg.at[r], lmsg.at[r], ml_s.at[r], ml_r.at[r])
-        go_left(msg.at[r], rmsg.at[r], mr_s.at[r], mr_r.at[r])
-        stay_first(msg.at[r], lmsg.at[r], ml_r.at[r])
-        stay_last(msg.at[r], rmsg.at[r], mr_r.at[r])
+        picked = pick_start(gram.at[0])
+        for h in range(2):
+
+            def two(i, carry):
+                now, carry = gram_step(gram.at[0], gram.at[1], carry)
+                msg[r, h, pl.ds(2 * i, 1)] = now
+                now, carry = gram_step(gram.at[1], gram.at[0], carry)
+                msg[r, h, pl.ds(2 * i + 1, 1)] = now
+                return carry
+
+            picked = lax.fori_loop(0, PART // 2, two, picked)
+            msg[r, h, PART:] = jnp.where(swap[:PART], 1.0, 0.0)
+            go_right(msg.at[r, h], lmsg.at[r, h], ml_s.at[r, h], ml_r.at[r, h])
+            go_left(msg.at[r, h], rmsg.at[r, h], mr_s.at[r, h], mr_r.at[r, h])
+            stay_first(msg.at[r, h], lmsg.at[r, h], ml_r.at[r, h])
+            stay_last(msg.at[r, h], rmsg.at[r, h], mr_r.at[r, h])
+        if r > 0:
+            forward(r, CHUNKS - 1)
 
         if r < ROUNDS - 1:
-            swaps = jnp.broadcast_to(msg[r, STEPS : STEPS + 1], (W, W)) > 0.5
+            swaps = jnp.broadcast_to(msg[r, 0, PART : PART + 1], (W, W)) > 0.5
             u, v = gram[0, 0, INNER], gram[0, 3, INNER]
             gx[r] = jnp.where(swaps, v, u)
             gy[r] = jnp.where(swaps, u, v)
@@ -326,10 +368,12 @@
             stay_last(gx.at[r], gb.at[r], gb_r.at[r])
             stay_first(gy.at[r], gt.at[r], gt_r.at[r])
 
-        rebuild([msg.at[r]], [base])
-        turn = split(jnp.concatenate(halves(msg.at[r], base), axis=0))
+        identity([base, base_l, base_r])
+        for h in range(2):
+            rebuild([msg.at[r, h]], [base])
+        turn = split(jnp.concatenate(halves(msg.at[r, 0], base), axis=0))
         for c in [*range(RAW, CHUNKS), *range(RAW)]:
-            at = slice(c * step, (c + 1) * step)
+            at = rows_of(c)
             new = times(top[r, at], bot[r, at], turn)
             xs[r, at] = new[:, :W]
             ys[r, at] = new[:, W:]
@@ -340,16 +384,19 @@
                 stay_first(ys.at[r, src], top.at[1, src], x_r.at[c])
                 stay_last(xs.at[r, src], bot.at[1, src], y_r.at[c])
 
-        arrived(lmsg.at[r], ml_r.at[r])
-        arrived(rmsg.at[r], mr_r.at[r])
-        rebuild([lmsg.at[r], rmsg.at[r]], [base_l, base_r])
-        turn_l = split(halves(lmsg.at[r], base_l)[0])
-        turn_r = split(halves(rmsg.at[r], base_r)[1])
-        at_first = jnp.broadcast_to(p, (step, W)) == 0
-        at_last = jnp.broadcast_to(p, (step, W)) == last
+        for h in range(2):
+            arrived(lmsg.at[r, h], ml_r.at[r, h])
+            arrived(rmsg.at[r, h], mr_r.at[r, h])
+            rebuild([lmsg.at[r, h], rmsg.at[r, h]], [base_l, base_r])
+        turn_l = split(halves(lmsg.at[r, 0], base_l)[0])
+        turn_r = split(halves(rmsg.at[r, 0], base_r)[1])
+        old = []
+        if r < ROUNDS - 1:
+            old = list(finish)
+            finish.clear()
         total = None
         for c in range(CHUNKS):
-            at = slice(c * step, (c + 1) * step)
+            at = rows_of(c)
             ref = part_of(c)
             if r == 0 and c >= RAW:
                 arrived(top.at[1, ref], x_r.at[c])
@@ -364,21 +411,28 @@
                     l_b, r_t = lb[at], rt[at]
                 else:
                     l_b, r_t = ys[r - 1, at], xs[r - 1, at]
+                at_first = jnp.broadcast_to(p, (sizes[c], W)) == 0
+                at_last = jnp.broadcast_to(p, (sizes[c], W)) == last
                 new_top = jnp.where(at_first, ys[r, at], times(ft[r, at], l_b, turn_l))
                 new_bot = jnp.where(at_last, xs[r, at], times(r_t, fb[r, at], turn_r))
                 if r < ROUNDS - 1:
                     top[r + 1, at] = new_top
                     bot[r + 1, at] = new_bot
                 else:
-                    out_top[at] = new_top
-                    out_bot[at] = new_bot
+                    for h, new in enumerate((new_top, new_bot)):
+                        done[h, at] = new
+                        copy = pltpu.make_async_copy(
+                            done.at[h, ref], out.at[ref, pl.ds(h * W, W)], out_sem.at[c, h])
+                        copy.start()
+                        finish.append(copy.wait)
             if r < ROUNDS - 1:
-                forward(r + 1, c)
+                if c < CHUNKS - 1:
+                    forward(r + 1, c)
                 now = cross_gram(new_top, new_bot)
                 total = now if c == 0 else total + now
         if r < ROUNDS - 1:
             part[r] = total
-            sum_small(r)
+            sum_small(r, old)
 
     for wait in finish:
         wait()
@@ -390,34 +444,36 @@
     R = ROUNDS
     C = CHUNKS
     dma = pltpu.SemaphoreType.DMA
-    half = jax.ShapeDtypeStruct((rows, W), F32)
 
     def vmem(*shape):
         return pltpu.VMEM(shape, F32)
 
-    top, bottom = pl.pallas_call(
+    return pl.pallas_call(
         kernel,
-        out_shape=(half, half),
+        out_shape=jax.ShapeDtypeStruct(matrix.shape, F32),
         in_specs=[pl.BlockSpec(memory_space=pl.ANY), pl.BlockSpec(memory_space=pltpu.VMEM)],
-        out_specs=(pl.BlockSpec(memory_space=pltpu.VMEM), pl.BlockSpec(memory_space=pltpu.VMEM)),
+        out_specs=pl.BlockSpec(memory_space=pl.ANY),
         scratch_shapes=[
+            vmem(2, rows, W),
             *(vmem(R, rows, W) for _ in range(6)),
             *(vmem(rows, W) for _ in range(2)),
             *(vmem(2, 4, W + 2 * PAD, W) for _ in range(4)),
-            vmem(2, W + H, W),
-            vmem(W + H, W),
-            vmem(n // 2, W + H, W),
-            vmem(2, W + H, W),
+            vmem(2, W + 8, W),
+            vmem(W + 8, W),
+            vmem(n // 2, W + 8, W),
+            vmem(2, W + 8, W),
             vmem(R - 1, W, W),
             vmem(R - 1, W, W),
             vmem(R - 1, n // 2, W, W),
             vmem(R - 1, W, W),
-            *(vmem(R, 2 * STEPS, W) for _ in range(3)),
+            *(vmem(R, 2, 2 * PART, W) for _ in range(3)),
             *(vmem(R - 1, W, W) for _ in range(4)),
+            dma((C, 2)),
             dma((C, 2)),
             *(dma((R, C)) for _ in range(4)),
             *(dma((C,)) for _ in range(8)),
-            *(dma((R,)) for _ in range(8)),
+            *(dma((R, 2)) for _ in range(4)),
+            *(dma((R,)) for _ in range(4)),
             dma((2,)),
             dma((2,)),
             dma((n // 2,)),
@@ -430,7 +486,6 @@
         compiler_params=pltpu.CompilerParams(
             collective_id=0, has_side_effects=True, vmem_limit_bytes=60 * 1024 * 1024),
     )(matrix, flips.T)
-    return jnp.concatenate([top, bottom], axis=1)
 
 
 def solution(mesh):

time: 81.1 us -> 80.6 us (level)
  local copies, waits for them, and re-layouts: 0 us -> 2.26 us
  other arithmetic: 2.24 us -> 0 us
    unnamed x0 -> x1, local copies, waits for them, and re-layouts: none -> 2.26 us
    concatenate x1 -> x0, other arithmetic: 2.24 us -> none  [body(): return jnp.concatenate([top, bottom], axis=1)]
where the time goes in v3:
time: 80.6 us; the launch traced here: 80.5 us
  Pallas kernels  78.2 us (97%)
  local copies, waits for them, and re-layouts  2.26 us (3%)
    pallas_call x1, Pallas kernels, body(): pl.pallas_call(kernel, out_shape=jax.ShapeDtypeStruct(matrix.shape, F32),...  78.2 us
    unnamed x1, local copies, waits for them, and re-layouts  2.26 us

profile of v3, /device:TPU:7, one launch (start us, length us, event | category | flops | bytes accessed | tf_op | source)
XLA Modules:
  0.0 80.5 jit_solution(6143171212930743957)
XLA Ops:
  0.0 78.2 %shard_map.28 = f32[1024,256]{1,0:T(8,128)} custom-call(f32[1024,256]{1,0:T(8,128)} %m_ref.1, s32[1,4]{1,0:T(1,128)} %bitcast.1), custom_call_target="tpu_custom_call" | custom-call | tf_op jit(solution)/shard_map/pallas_call | solution.py:451
  78.2 2.3 %copy.4 = f32[1024,256]{1,0:T(8,128)} copy(f32[1024,256]{1,0:T(8,128)} %shard_map.28) | data formatting | bytes 2097152

commit v4 on v3

--- a/solution.py
+++ b/solution.py
@@ -10,9 +10,10 @@
 W = 128
 H = W // 2
 PAD = 8
-SIZES = (320, 320, 192, 192)
+SIZES = (512, 384, 128)
 CHUNKS = len(SIZES)
-RAW = 2
+RAW = 1
+HELD = 1
 PART = STEPS // 2
 MESH = pl.DeviceIdType.MESH
 F32 = jnp.float32
@@ -42,7 +43,28 @@
 
 def times(t, b, turn):
     high, low = split(jnp.concatenate([t, b], axis=1))
-    return dot(high, turn[0], 1, 1) + (dot(high, turn[1], 1, 1) + dot(low, turn[0], 1, 1))
+    wide = turn.shape[0] // 2
+    both = dot(high, turn, 1, 1)
+    return both[:, :wide] + (both[:, wide:] + dot(low, turn[:wide], 1, 1))
+
+
+def side_gram(left, right):
+    lh, ll = split(left)
+    rh, rl = split(right)
+    return dot(lh, rh, 0, 0) + (dot(lh, rl, 0, 0) + dot(ll, rh, 0, 0))
+
+
+def turned_gram(turn_l, mid, turn_r):
+    high, low = split(mid)
+    first = dot(turn_l, high, 1, 0)
+    first = first[:W] + (first[W:] + dot(turn_l[:W], low, 1, 0))
+    high, low = split(first)
+    second = dot(high, turn_r, 1, 1)
+    return second[:, :W] + (second[:, W:] + dot(low, turn_r[:W], 1, 1))
+
+
+def stacked(x):
+    return jnp.concatenate(split(x), axis=0)
 
 
 def cos_sin(tangent):
@@ -172,10 +194,11 @@
     return right, left
 
 
-def kernel(m_ref, flips_ref, out, done, top, bot, xs, ys, ft, fb, lb, rt, gram, base, base_l, base_r,
+def kernel(m_ref, flips_ref, out, done, top, bot, xs, ys, ft, fb, lb, rt, gram, base, base_l, base_r, mid,
            part0, sib0, slabs0, sum0, part, sib, slabs, cross, msg, lmsg, rmsg, gx, gy, gt, gb,
            in_sem, out_sem, ft_s, ft_r, fb_s, fb_r, lb_s, lb_r, rt_s, rt_r, x_s, x_r, y_s, y_r,
-           ml_s, ml_r, mr_s, mr_r, gx_s, gt_r, gy_s, gb_r, one_s, one_r, far0_s, far0_r, sib_s, sib_r, far_s, far_r):
+           ml_s, ml_r, mr_s, mr_r, gx_s, gt_r, gy_s, gb_r, one_s, one_r, far0_s, far0_r, sib_s, sib_r, far_s, far_r,
+           sg_s, sg_r):
     p = lax.axis_index("col")
     q = lax.axis_index("row")
     last = lax.axis_size("col") - 1
@@ -189,6 +212,7 @@
     right = {"col": p + 1}
     left = {"col": p - 1}
     finish = []
+    mine = pl.ds(pl.multiple_of(core * H, H), H)
 
     def others(d):
         return {"row": lax.rem(q + 2 * d, n)}
@@ -263,9 +287,10 @@
         for copy in [near, back] + far:
             finish.append(copy.wait_send)
 
-    def sum_small(r, old):
+    def sum_small(r, between, during):
         near = remote(part.at[r], sib.at[r], sib_s.at[r], sib_r.at[r], sibling)
         near.start()
+        between()
         near.wait_recv()
         slabs[r, chip] = part[r] + sib[r]
         far = [
@@ -274,8 +299,7 @@
         ]
         for copy in far:
             copy.start()
-        for wait in old:
-            wait()
+        during()
         for copy in far:
             copy.wait_recv()
         total = slabs[r, 0]
@@ -331,8 +355,9 @@
             g_tt = jnp.where(row <= col, both, both_t)
             g_bb = jnp.where(row > col, both, jnp.where(row < col, both_t, ends))
         else:
-            arrived(gt.at[r - 1], gt_r.at[r - 1])
-            arrived(gb.at[r - 1], gb_r.at[r - 1])
+            for copy in shares:
+                copy.wait_recv()
+                finish.append(copy.wait_send)
             g_tt, g_bb, g_tb = gt[r - 1], gb[r - 1], cross[r - 1]
         for k, value in enumerate((g_tt, g_tb, g_tb.T, g_bb)):
             gram[0, k, INNER] = value
@@ -356,83 +381,138 @@
             stay_first(msg.at[r, h], lmsg.at[r, h], ml_r.at[r, h])
             stay_last(msg.at[r, h], rmsg.at[r, h], mr_r.at[r, h])
         if r > 0:
-            forward(r, CHUNKS - 1)
+            for c in range(CHUNKS - HELD, CHUNKS):
+                forward(r, c)
 
         if r < ROUNDS - 1:
             swaps = jnp.broadcast_to(msg[r, 0, PART : PART + 1], (W, W)) > 0.5
             u, v = gram[0, 0, INNER], gram[0, 3, INNER]
             gx[r] = jnp.where(swaps, v, u)
             gy[r] = jnp.where(swaps, u, v)
-            go_right(gx.at[r], gt.at[r], gx_s.at[r], gt_r.at[r])
-            go_left(gy.at[r], gb.at[r], gy_s.at[r], gb_r.at[r])
-            stay_last(gx.at[r], gb.at[r], gb_r.at[r])
-            stay_first(gy.at[r], gt.at[r], gt_r.at[r])
-
+            go_right(gx.at[r, mine], gt.at[r, mine], gx_s.at[r], gt_r.at[r])
+            go_left(gy.at[r, mine], gb.at[r, mine], gy_s.at[r], gb_r.at[r])
+            stay_last(gx.at[r, mine], gb.at[r, mine], gb_r.at[r])
+            stay_first(gy.at[r, mine], gt.at[r, mine], gt_r.at[r])
+
+        final = r == ROUNDS - 1
         identity([base, base_l, base_r])
-        for h in range(2):
-            rebuild([msg.at[r, h]], [base])
-        turn = split(jnp.concatenate(halves(msg.at[r, 0], base), axis=0))
-        for c in [*range(RAW, CHUNKS), *range(RAW)]:
+        if not final:
+            for h in range(2):
+                rebuild([msg.at[r, h]], [base])
+            turn = stacked(jnp.concatenate(halves(msg.at[r, 0], base), axis=0))
+            for c in [*range(RAW, CHUNKS), *range(RAW)]:
+                at = rows_of(c)
+                new = times(top[r, at], bot[r, at], turn)
+                xs[r, at] = new[:, :W]
+                ys[r, at] = new[:, W:]
+                if r == 0 and c >= RAW:
+                    src = part_of(c)
+                    go_right(xs.at[r, src], top.at[1, src], x_s.at[c], x_r.at[c])
+                    go_left(ys.at[r, src], bot.at[1, src], y_s.at[c], y_r.at[c])
+                    stay_first(ys.at[r, src], top.at[1, src], x_r.at[c])
+                    stay_last(xs.at[r, src], bot.at[1, src], y_r.at[c])
+
+        raw = range(RAW if r == 0 else CHUNKS)
+        late = [c for c in raw if r > 0 and c >= CHUNKS - HELD]
+
+        def wait_raw(c):
+            ref = part_of(c)
+            arrived(ft.at[r, ref], ft_r.at[r, c])
+            arrived(fb.at[r, ref], fb_r.at[r, c])
+            if r == 0:
+                arrived(lb.at[ref], lb_r.at[c])
+                arrived(rt.at[ref], rt_r.at[c])
+
+        def sides(c):
             at = rows_of(c)
-            new = times(top[r, at], bot[r, at], turn)
-            xs[r, at] = new[:, :W]
-            ys[r, at] = new[:, W:]
-            if r == 0 and c >= RAW:
-                src = part_of(c)
-                go_right(xs.at[r, src], top.at[1, src], x_s.at[c], x_r.at[c])
-                go_left(ys.at[r, src], bot.at[1, src], y_s.at[c], y_r.at[c])
-                stay_first(ys.at[r, src], top.at[1, src], x_r.at[c])
-                stay_last(xs.at[r, src], bot.at[1, src], y_r.at[c])
+            if r == 0:
+                l_b, r_t = lb[at], rt[at]
+            else:
+                l_b = jnp.where(jnp.broadcast_to(p, (sizes[c], W)) == 0, bot[r, at], ys[r - 1, at])
+                r_t = jnp.where(jnp.broadcast_to(p, (sizes[c], W)) == last, top[r, at], xs[r - 1, at])
+            return jnp.concatenate([ft[r, at], l_b], axis=1), jnp.concatenate([r_t, fb[r, at]], axis=1)
+
+        def add_sides(c):
+            wait_raw(c)
+            now = side_gram(*sides(c))
+            mid[...] = now if c == 0 else mid[...] + now
+
+        def make(c):
+            at, ref = rows_of(c), part_of(c)
+            l_pair, r_pair = sides(c)
+            news = times(l_pair[:, :W], l_pair[:, W:], turn_l), times(r_pair[:, :W], r_pair[:, W:], turn_r)
+            if not final:
+                top[r + 1, at], bot[r + 1, at] = news
+                if c < CHUNKS - HELD:
+                    forward(r + 1, c)
+                return
+            for h, new in enumerate(news):
+                done[h, at] = new
+                copy = pltpu.make_async_copy(done.at[h, ref], out.at[ref, pl.ds(h * W, W)], out_sem.at[c, h])
+                copy.start()
+                finish.append(copy.wait)
+
+        for c in raw:
+            if c not in late:
+                if final:
+                    wait_raw(c)
+                else:
+                    add_sides(c)
 
         for h in range(2):
             arrived(lmsg.at[r, h], ml_r.at[r, h])
             arrived(rmsg.at[r, h], mr_r.at[r, h])
             rebuild([lmsg.at[r, h], rmsg.at[r, h]], [base_l, base_r])
-        turn_l = split(halves(lmsg.at[r, 0], base_l)[0])
-        turn_r = split(halves(rmsg.at[r, 0], base_r)[1])
-        old = []
-        if r < ROUNDS - 1:
-            old = list(finish)
-            finish.clear()
-        total = None
-        for c in range(CHUNKS):
-            at = rows_of(c)
-            ref = part_of(c)
-            if r == 0 and c >= RAW:
+        goes, stays = halves(lmsg.at[r, 0], base_l)
+        turn_l = stacked(jnp.where(jnp.broadcast_to(p, goes.shape) == 0, stays, goes))
+        stays, goes = halves(rmsg.at[r, 0], base_r)
+        turn_r = stacked(jnp.where(jnp.broadcast_to(p, goes.shape) == last, stays, goes))
+
+        if final:
+            for c in raw:
+                if c in late:
+                    wait_raw(c)
+                make(c)
+            continue
+
+        old = list(finish)
+        finish.clear()
+        make(0)
+        for c in late:
+            add_sides(c)
+        total = turned_gram(turn_l, mid[...], turn_r)
+        if r == 0:
+            for c in range(RAW, CHUNKS):
+                at, ref = rows_of(c), part_of(c)
                 arrived(top.at[1, ref], x_r.at[c])
                 arrived(bot.at[1, ref], y_r.at[c])
-                new_top, new_bot = top[1, at], bot[1, at]
+                total = total + cross_gram(top[1, at], bot[1, at])
+        part[r] = total
+
+        def between():
+            if r == 0:
+                for c in range(RAW, CHUNKS - HELD):
+                    forward(1, c)
             else:
-                arrived(ft.at[r, ref], ft_r.at[r, c])
-                arrived(fb.at[r, ref], fb_r.at[r, c])
-                if r == 0:
-                    arrived(lb.at[ref], lb_r.at[c])
-                    arrived(rt.at[ref], rt_r.at[c])
-                    l_b, r_t = lb[at], rt[at]
-                else:
-                    l_b, r_t = ys[r - 1, at], xs[r - 1, at]
-                at_first = jnp.broadcast_to(p, (sizes[c], W)) == 0
-                at_last = jnp.broadcast_to(p, (sizes[c], W)) == last
-                new_top = jnp.where(at_first, ys[r, at], times(ft[r, at], l_b, turn_l))
-                new_bot = jnp.where(at_last, xs[r, at], times(r_t, fb[r, at], turn_r))
-                if r < ROUNDS - 1:
-                    top[r + 1, at] = new_top
-                    bot[r + 1, at] = new_bot
-                else:
-                    for h, new in enumerate((new_top, new_bot)):
-                        done[h, at] = new
-                        copy = pltpu.make_async_copy(
-                            done.at[h, ref], out.at[ref, pl.ds(h * W, W)], out_sem.at[c, h])
-                        copy.start()
-                        finish.append(copy.wait)
-            if r < ROUNDS - 1:
-                if c < CHUNKS - 1:
-                    forward(r + 1, c)
-                now = cross_gram(new_top, new_bot)
-                total = now if c == 0 else total + now
-        if r < ROUNDS - 1:
-            part[r] = total
-            sum_small(r, old)
+                make(1)
+
+        shares = [
+            remote(buf.at[r, mine], buf.at[r, mine], sg_s.at[r, k], sg_r.at[r, k], sibling)
+            for k, buf in enumerate((gt, gb))
+        ]
+
+        def during():
+            arrived(gt.at[r, mine], gt_r.at[r])
+            arrived(gb.at[r, mine], gb_r.at[r])
+            for copy in shares:
+                copy.start()
+            if r > 0:
+                for c in range(2, CHUNKS):
+                    make(c)
+            for wait in old:
+                wait()
+
+        sum_small(r, between, during)
 
     for wait in finish:
         wait()
@@ -458,6 +538,7 @@
             *(vmem(R, rows, W) for _ in range(6)),
             *(vmem(rows, W) for _ in range(2)),
             *(vmem(2, 4, W + 2 * PAD, W) for _ in range(4)),
+            vmem(2 * W, 2 * W),
             vmem(2, W + 8, W),
             vmem(W + 8, W),
             vmem(n // 2, W + 8, W),
@@ -482,6 +563,8 @@
             dma((R,)),
             dma((R, n // 2)),
             dma((R, n // 2)),
+            dma((R, 2)),
+            dma((R, 2)),
         ],
         compiler_params=pltpu.CompilerParams(
             collective_id=0, has_side_effects=True, vmem_limit_bytes=60 * 1024 * 1024),

time: 80.6 us -> 75.8 us (0.940)
  Pallas kernels: 78.2 us -> 73.4 us
    pallas_call x1, Pallas kernels: 78.2 us -> 73.4 us  [body(): pl.pallas_call(kernel, out_shape=jax.ShapeDtypeStruct(matrix.shape, F32),...]
where the time goes in v4:
time: 75.8 us; the launch traced here: 75.7 us
  Pallas kernels  73.4 us (97%)
  local copies, waits for them, and re-layouts  2.26 us (3%)
    pallas_call x1, Pallas kernels, body(): pl.pallas_call(kernel, out_shape=jax.ShapeDtypeStruct(matrix.shape, F32),...  73.4 us
    unnamed x1, local copies, waits for them, and re-layouts  2.26 us

profile of v4, /device:TPU:7, one launch (start us, length us, event | category | flops | bytes accessed | tf_op | source)
XLA Modules:
  0.0 75.7 jit_solution(10965867755237315954)
XLA Ops:
  0.0 73.4 %shard_map.28 = f32[1024,256]{1,0:T(8,128)} custom-call(f32[1024,256]{1,0:T(8,128)} %m_ref.1, s32[1,4]{1,0:T(1,128)} %bitcast.1), custom_call_target="tpu_custom_call" | custom-call | tf_op jit(solution)/shard_map/pallas_call | solution.py:531
  73.4 2.3 %copy.4 = f32[1024,256]{1,0:T(8,128)} copy(f32[1024,256]{1,0:T(8,128)} %shard_map.28) | data formatting | bytes 2097152

commit v5 on v4

--- a/solution.py
+++ b/solution.py
@@ -10,7 +10,7 @@
 W = 128
 H = W // 2
 PAD = 8
-SIZES = (512, 384, 128)
+SIZES = (448, 448, 128)
 CHUNKS = len(SIZES)
 RAW = 1
 HELD = 1
@@ -212,6 +212,7 @@
     right = {"col": p + 1}
     left = {"col": p - 1}
     finish = []
+    far_order = sorted(range(1, n // 2), key=lambda d: -min(d, n // 2 - d))
     mine = pl.ds(pl.multiple_of(core * H, H), H)
 
     def others(d):
@@ -271,7 +272,7 @@
         slabs0[chip] = part0[core] + sib0[...]
         far = [
             remote(slabs0.at[chip], slabs0.at[chip], far0_s.at[d], far0_r.at[d], others(d))
-            for d in range(1, n // 2)
+            for d in far_order
         ]
         for copy in far:
             copy.start()
@@ -295,7 +296,7 @@
         slabs[r, chip] = part[r] + sib[r]
         far = [
             remote(slabs.at[r, chip], slabs.at[r, chip], far_s.at[r, d], far_r.at[r, d], others(d))
-            for d in range(1, n // 2)
+            for d in far_order
         ]
         for copy in far:
             copy.start()
@@ -459,6 +460,10 @@
                 else:
                     add_sides(c)
 
+        if final:
+            for wait in finish:
+                wait()
+            finish.clear()
         for h in range(2):
             arrived(lmsg.at[r, h], ml_r.at[r, h])
             arrived(rmsg.at[r, h], mr_r.at[r, h])
@@ -567,7 +572,7 @@
             dma((R, 2)),
         ],
         compiler_params=pltpu.CompilerParams(
-            collective_id=0, has_side_effects=True, vmem_limit_bytes=60 * 1024 * 1024),
+            collective_id=0, has_side_effects=True, vmem_limit_bytes=46 * 1024 * 1024),
     )(matrix, flips.T)
 
 

time: 75.8 us -> 73.7 us (0.972)
  Pallas kernels: 73.4 us -> 70.2 us
    pallas_call x1, Pallas kernels: 73.4 us -> 70.2 us  [body(): pl.pallas_call(kernel, out_shape=jax.ShapeDtypeStruct(matrix.shape, F32),...]
    unnamed x1 -> x5, local copies, waits for them, and re-layouts: 2.26 us -> 2.85 us
where the time goes in v5:
time: 73.7 us; the launch traced here: 73 us
  Pallas kernels  70.2 us (95%)
  local copies, waits for them, and re-layouts  2.85 us (4%)
    pallas_call x1, Pallas kernels, body(): pl.pallas_call(kernel, out_shape=jax.ShapeDtypeStruct(matrix.shape, F32),...  70.2 us
    unnamed x5, local copies, waits for them, and re-layouts  2.85 us

profile of v5, /device:TPU:7, one launch (start us, length us, event | category | flops | bytes accessed | tf_op | source)
XLA Modules:
  0.0 73.0 jit_solution(10469264320462488239)
XLA Ops:
  0.0 0.0 copy-start.1
  0.0 0.7 copy-done.1
  0.7 0.0 copy-start
  0.7 1.2 %copy-done = f32[1024,256]{1,0:T(8,128)S(1)} copy-done((f32[1024,256]{1,0:T(8,128)S(1)}, f32[1024,256]{1,0:T(8,128)}, u32[]{:S(2)}) %copy-start) | copy-done | bytes 1048600
  1.9 70.2 %shard_map.28 = f32[1024,256]{1,0:T(8,128)S(1)} custom-call(f32[1024,256]{1,0:T(8,128)S(1)} %copy-done, s32[1,4]{1,0:T(1,128)S(1)} %bitcast.1), custom_call_target="tpu_custom_call" | custom-call | tf_op jit(solution)/shard_map/pallas_call | solution.py:536
  72.1 1.0 %copy.4 = f32[1024,256]{1,0:T(8,128)} copy(f32[1024,256]{1,0:T(8,128)S(1)} %shard_map.28) | data formatting | bytes 2097152
Async XLA Ops:
  0.0 0.7 copy-start.1
  0.7 1.2 %copy-start = (f32[1024,256]{1,0:T(8,128)S(1)}, f32[1024,256]{1,0:T(8,128)}, u32[]{:S(2)}) copy-start(f32[1024,256]{1,0:T(8,128)} %m_ref.1) | copy-start | bytes 3145732
